TPU v7x, 32 devices: a whole 2x2x4 slice. The times are simulated.
32 devices in a mesh: row: 8 (over z, core), col: 4 (over y, x).
Axes of the slice: x: 2, y: 2, z: 4, core: 2. Of those that a mesh axis runs over, the one named last changes fastest.
Arguments:
- gradient: bfloat16 [8192, 26624], P('row', 'col'), may hold values from -128 to 128
- momentum: bfloat16 [8192, 26624], P('row', 'col'), may hold values from -6 to 6
- weight: bfloat16 [8192, 26624], P('row', 'col'), may hold values from -6 to 6
- right_factor: float32 [26624, 256], P('col'), may hold values from -6 to 6
Outputs:
- new_weight: bfloat16 [8192, 26624], P('row', 'col')
- new_momentum: bfloat16 [8192, 26624], P('row', 'col')
- new_factor: float32 [26624, 256], P('col')
All inputs are finite; a program needn't handle non-finite values.
Results may differ from a plain program's by a relative error of at most 0.0015.
Values sent between devices are 32-bit elements; how exact they have to be, the bound alone decides.
A program may use at most 128 MiB of HBM per device.

v0:
```python
import jax
import jax.numpy as jnp
from jax import lax
from jax.sharding import PartitionSpec as P

ROWS = 8192
COLS = 26624
RANK = 256


decay = 0.95
step_size = 0.3


def factor_gram(gram):
    rank = gram.shape[0]
    jitter = 1e-06 * jnp.trace(gram) / rank
    return jnp.linalg.cholesky(gram + jitter * jnp.eye(rank, dtype=jnp.float32))


def solve_right(block, chol):
    return lax.linalg.triangular_solve(chol, block, left_side=False, lower=True, transpose_a=True)


def cross_product(buffer, source):
    return lax.dot_general(
        buffer, source, (((0,), (0,)), ((), ())), precision=lax.Precision.HIGHEST
    )


def gram_of(left):
    return jnp.dot(left.T, left, precision=lax.Precision.HIGHEST)


def gram_total(left):
    return lax.psum(gram_of(left), "row")


def local(gradient, momentum, weight, right_factor):
    high = lax.Precision.HIGHEST
    buffer = momentum.astype(jnp.float32) + gradient.astype(jnp.float32)
    left = lax.psum(jnp.dot(buffer, right_factor, precision=high), "col")
    chol = factor_gram(gram_total(left))
    ortho = solve_right(left, chol)
    right_part = lax.psum(cross_product(buffer, ortho), "row")
    squares = lax.psum(jnp.sum(right_part * right_part, axis=0), "col")
    new_momentum = (buffer - (1.0 - decay) * jnp.dot(ortho, right_part.T, precision=high)).astype(
        jnp.bfloat16
    )
    new_factor = right_part / jnp.sqrt(squares / COLS + 1e-06)
    update = jnp.dot(ortho, new_factor.T, precision=high)
    new_weight = (weight.astype(jnp.float32) - step_size * jnp.sqrt(ROWS / RANK) * update).astype(
        jnp.bfloat16
    )
    return (new_weight, new_momentum, new_factor)


def solution(mesh):
    in_specs = (P("row", "col"), P("row", "col"), P("row", "col"), P("col", None))
    out_specs = (P("row", "col"), P("row", "col"), P("col", None))
    return jax.shard_map(local, mesh=mesh, in_specs=in_specs, out_specs=out_specs, check_vma=False)
```

profile of v0, /device:TPU:0, one launch (start us, length us, event | category | flops | bytes accessed | tf_op | source)
XLA Modules:
  0.0 539.9 jit_solution(18347098700334435987)
XLA Ops:
  7.2 0.0 all-reduce.5.cloned.1.call-start
  7.2 28.5 %fusion.1 = f32[1024,256]{1,0:T(8,128)} fusion(f32[6656,256]{1,0:T(8,128)} %param.7, bf16[1024,6656]{1,0:T(8,128)(2,1)} %param.4, bf16[1024,6656]{1,0:T(8,128)(2,1)} %param.5), kind=kOutput, calls=%fused_computation.6 | convolution fusion | flops 20958412800 | bytes 35127296 | tf_op jit(solution)/shard_map/dot_general | solution.py:42
  35.7 0.0 all-reduce.5.cloned.1.call-update
  35.7 0.0 all-reduce.7.cloned.1.call-start
  35.7 55.4 %all-reduce.5.cloned.1.call-done = f32[1024,256]{1,0:T(8,128)} async-done(((f32[1024,256]{1,0:T(8,128)}), f32[1024,256]{1,0:T(8,128)}) %all-reduce.5.cloned.1.call-update) | async-done | bytes 1048592 | tf_op jit(solution)/shard_map/psum | solution.py:42
  91.1 4.1 fusion.14
  95.2 0.0 all-reduce.7.cloned.1.call-update
  95.2 0.2 all-reduce.9.cloned.1.call-start
  95.4 54.8 %all-reduce.7.cloned.1.call-done = f32[256,256]{0,1:T(8,128)} async-done(((f32[256,256]{0,1:T(8,128)}), f32[256,256]{0,1:T(8,128)}) %all-reduce.7.cloned.1.call-update) | async-done | bytes 262160 | tf_op jit(solution)/shard_map/psum | solution.py:36
  150.3 1.6 select_reduce_fusion
  152.5 1.0 select_add_fusion
  153.5 0.1 copy.8
  153.6 1.0 fusion.4
  154.6 11.7 %cholesky.49 = f32[128,128]{1,0:T(8,128)S(1)} custom-call(f32[128,128]{1,0:T(8,128)S(1)} %cholesky.115), custom_call_target="Cholesky" | custom-call | tf_op jit(solution)/shard_map/jit(cholesky)/cholesky | solution.py:18
  166.3 0.1 copy.9
  166.5 9.8 %custom-call.14 = f32[1,128,128]{1,2,0:T(8,128)S(1)} custom-call(f32[1,128,128]{2,1,0:T(8,128)S(1)} %get-tuple-element.26), custom_call_target="InvertDiagBlocksLowerTriangular" | custom-call | tf_op jit(solution)/shard_map/jit(cholesky)/cholesky | solution.py:18
  176.3 0.2 fusion.7
  176.5 0.3 convolution_subtract_fusion.1
  176.8 0.1 copy.10
  176.9 11.7 %cholesky.103 = f32[128,128]{1,0:T(8,128)S(1)} custom-call(f32[128,128]{1,0:T(8,128)S(1)} %convolution_subtract_fusion.1), custom_call_target="Cholesky" | custom-call | tf_op jit(solution)/shard_map/jit(cholesky)/cholesky | solution.py:18
  188.6 0.1 copy.11
  188.7 0.6 compare_reduce_fusion
  190.8 0.1 triangular_solve.63
  190.8 4.2 while.1
  190.8 0.6 fusion.25
  191.4 1.4 dynamic-slice.7
  192.8 0.1 copy.16
  193.0 0.6 fusion.25
  193.5 1.4 dynamic-slice.7
  194.9 0.1 copy.16
  195.1 19.7 %custom-call.15 = f32[2,128,128]{1,2,0:T(8,128)S(1)} custom-call(f32[2,128,128]{2,1,0:T(8,128)S(1)} %get-tuple-element.10), custom_call_target="InvertDiagBlocksLowerTriangular" | custom-call | tf_op jit(solution)/shard_map/triangular_solve | solution.py:22
  214.7 1.7 fusion.2
  216.4 2.0 convolution_subtract_fusion
  218.5 0.6 fusion.5
  219.1 0.0 copy-start.1
  219.1 0.8 copy-done.1
  219.9 48.1 %fusion = f32[6656,256]{1,0:T(8,128)} fusion(bf16[1024,6656]{1,0:T(8,128)(2,1)} %param.4, bf16[1024,6656]{1,0:T(8,128)(2,1)} %param.5, f32[1024,128]{0,1:T(8,128)S(1)} %fusion.5, f32[1024,128]{0,1:T(8,128)S(1)} %fusion.2), kind=kOutput, calls=%fused_computation.5 | convolution fusion | flops 20958674944 | bytes 35127296 | tf_op jit(solution)/shard_map/dot_general | solution.py:26
  268.0 0.0 all-reduce.9.cloned.1.call-update
  268.0 145.1 %all-reduce.9.cloned.1.call-done = f32[6656,256]{1,0:T(8,128)} async-done(((f32[6656,256]{1,0:T(8,128)}), f32[6656,256]{1,0:T(8,128)}) %all-reduce.9.cloned.1.call-update) | async-done | bytes 6815760 | tf_op jit(solution)/shard_map/psum | solution.py:45
  413.1 3.8 multiply_reduce_fusion
  416.9 10.0 %psum.31 = f32[256]{0:T(256)S(1)} all-reduce(f32[256]{0:T(256)S(1)} %multiply_reduce_fusion), channel_id=1, replica_groups=mesh['row'=8,'col'=4] {'col'}, use_global_device_ids=true, to_apply=%region_9.10 | all-reduce | flops 256 | bytes 2048 | tf_op jit(solution)/shard_map/psum | solution.py:46
  426.9 3.6 broadcast_divide_fusion
  430.5 0.0 copy-start
  430.5 0.0 slice-start.1
  430.5 50.5 %subtract_convert_fusion.1 = bf16[1024,6656]{1,0:T(8,128)(2,1)} fusion(bf16[1024,6656]{1,0:T(8,128)(2,1)} %param.6, f32[6656,256]{1,0:T(8,128)S(1)} %broadcast_divide_fusion, f32[1024,128]{0,1:T(8,128)} %copy-done.1, f32[1024,128]{0,1:T(8,128)S(1)} %fusion.2), kind=kOutput, calls=%fused_computation.3 | convolution fusion | flops 20965490688 | bytes 35127296 | tf_op jit(solution)/shard_map/dot_general | solution.py:51
  481.0 0.0 copy-done
  481.0 0.0 slice-done
  481.0 52.2 %subtract_convert_fusion = bf16[1024,6656]{1,0:T(8,128)(2,1)} fusion(bf16[1024,6656]{1,0:T(8,128)(2,1)} %param.4, bf16[1024,6656]{1,0:T(8,128)(2,1)} %param.5, f32[6656,256]{1,0:T(8,128)S(1)} %bitcast.35, f32[1024,128]{0,1:T(8,128)} %copy-done.1, f32[1024,128]{0,1:T(8,128)S(1)} %fusion.2), kind=kOutput, calls=%fused_computation.2 | convolution fusion | flops 20979122176 | bytes 48758784 | tf_op jit(solution)/shard_map/dot_general | solution.py:47
  (17 shorter events, 0.2 us)
Async XLA Ops:
  7.2 83.9 %all-reduce.5.cloned.1.call-start = ((), (), s32[]{:S(2)}) async-start(), calls=%async_computation | async-start | bytes 2097152 | tf_op jit(solution)/shard_map/psum | solution.py:42
  35.7 114.6 %all-reduce.7.cloned.1.call-start = ((), (), s32[]{:S(2)}) async-start(), calls=%async_computation.1 | async-start | bytes 524288 | tf_op jit(solution)/shard_map/psum | solution.py:36
  95.2 317.9 %all-reduce.9.cloned.1.call-start = ((), (), s32[]{:S(2)}) async-start(), calls=%async_computation.2 | async-start | bytes 13631488 | tf_op jit(solution)/shard_map/psum | solution.py:45
  219.1 0.8 copy-start.1
  426.9 54.1 %slice-start = ((s8[6815744]{0:T(1024)(128)(4,1)}), s8[4194304]{0:T(1024)(128)(4,1)S(1)}, s32[]{:S(2)}) async-start(s8[6815744]{0:T(1024)(128)(4,1)} %bitcast.34), calls=%async_computation.3 | async-start | bytes 8388608
  430.5 50.5 %copy-start = (f32[6656,256]{1,0:T(8,128)}, f32[6656,256]{1,0:T(8,128)S(1)}, u32[]{:S(2)}) copy-start(f32[6656,256]{1,0:T(8,128)S(1)} %broadcast_divide_fusion) | copy-start | bytes 20447236
  430.5 50.5 %slice-start.1 = ((s8[6815744]{0:T(1024)(128)(4,1)}), s8[2621440]{0:T(1024)(128)(4,1)S(1)}, s32[]{:S(2)}) async-start(s8[6815744]{0:T(1024)(128)(4,1)} %bitcast.34), calls=%async_computation.4 | async-start | bytes 5242880
Sparse Core Ops, SparseCore 0:
  35.8 55.2 all-reduce.4
  95.3 54.8 all-reduce.6
  268.1 144.8 all-reduce.8
where the time goes:
time: 546 us; the launch traced here: 540 us
  waiting for transfers between devices  255 us (47%)
  matrix products  188 us (34%)
  other arithmetic  64.6 us (12%)
  between operations  16.1 us (3%)
  blocking collectives  10 us (2%)
  local copies, waits for them, and re-layouts  5.5 us (1%)
    psum x1, waiting for transfers between devices, local(): right_part = lax.psum(cross_product(buffer, ortho), 'row')  145 us
    psum x1, waiting for transfers between devices, local(): left = lax.psum(jnp.dot(buffer, right_factor, precision=high), 'col')  55.4 us
    psum x1, waiting for transfers between devices, gram_total(): return lax.psum(gram_of(left), 'row')  54.8 us
    dot_general x1, matrix products, local(): jnp.dot(ortho, right_part.T, precision=high)  52.2 us
    dot_general x1, matrix products, local(): update = jnp.dot(ortho, new_factor.T, precision=high)  50.5 us
    dot_general x1, matrix products, cross_product(): lax.dot_general(buffer, source, (((0,), (0,)), ((), ())), precision=lax.P...  48.1 us
    another operation x6, other arithmetic, factor_gram(): return jnp.linalg.cholesky(gram + jitter * jnp.eye(rank, dtype=jnp.float32))  34 us
    dot_general x1, matrix products, local(): left = lax.psum(jnp.dot(buffer, right_factor, precision=high), 'col')  28.5 us
  transfers between devices with their start and end apart: 3, of which 3 were waited for; matrix products, arithmetic and copies ran while one was open for 0% of the time, Pallas kernels for 0%

commit v1 on v0

v1 whole, which is shorter than its diff:
```python
import functools

import jax
import jax.numpy as jnp
from jax import lax
from jax.experimental import pallas as pl
from jax.experimental.pallas import tpu as pltpu
from jax.sharding import PartitionSpec as P

ROWS = 8192
COLS = 26624
RANK = 256

decay = 0.95
step_size = 0.3

MESH = pl.DeviceIdType.MESH
HIGH = lax.Precision.HIGHEST
F32 = jnp.float32
BF16 = jnp.bfloat16
VMEM = pltpu.VMEM
DMA = pltpu.SemaphoreType.DMA
LIMIT = 56 * 1024 * 1024


def split(x):
    hi = x.astype(BF16)
    return hi, (x - hi.astype(F32)).astype(BF16)


def mm(a, b):
    return jnp.dot(a, b, preferred_element_type=F32)


def tile_of(cols):
    for tile in (512, 256, 128):
        if cols % tile == 0:
            return tile
    return cols


def whole(shape):
    return pl.BlockSpec(shape, lambda i: (0,) * len(shape))


def left_kernel(g_ref, m_ref, r_ref, out_ref):
    @pl.when(pl.program_id(0) == 0)
    def _():
        out_ref[...] = jnp.zeros_like(out_ref)

    b_hi, b_lo = split(g_ref[...].astype(F32) + m_ref[...].astype(F32))
    r_hi, r_lo = split(r_ref[...])
    out_ref[...] += mm(b_hi, r_hi) + mm(b_lo, r_hi) + mm(b_hi, r_lo)


def left_part(g, m, r):
    rows, cols = g.shape
    tile = tile_of(cols)
    return pl.pallas_call(
        left_kernel,
        grid=(cols // tile,),
        in_specs=[
            pl.BlockSpec((rows, tile), lambda i: (0, i)),
            pl.BlockSpec((rows, tile), lambda i: (0, i)),
            pl.BlockSpec((tile, RANK), lambda i: (i, 0)),
        ],
        out_specs=whole((rows, RANK)),
        out_shape=jax.ShapeDtypeStruct((rows, RANK), F32),
        compiler_params=pltpu.CompilerParams(vmem_limit_bytes=LIMIT),
    )(g, m, r)


def greet(peers):
    barrier = pltpu.get_barrier_semaphore()
    for peer in peers:
        pl.semaphore_signal(barrier, inc=1, device_id=peer, device_id_type=MESH)
    return barrier


def sums_kernel(nr, nc, part, left, gram, l_in, g_part, g_in, ls, lr, las, lar, gs, gr, gas, gar):
    ri, ci = lax.axis_index("row"), lax.axis_index("col")
    cols = [lax.rem(ci + d, nc) for d in range(nc)]
    rows = [lax.rem(ri + d, nr) for d in range(nr)]
    barrier = greet([{"col": p} for p in cols[1:]] + [{"row": p} for p in rows[1:]])
    pl.semaphore_wait(barrier, nc + nr - 2)

    def copy(src, dst, send, recv, peer):
        return pltpu.make_async_remote_copy(
            src_ref=src, dst_ref=dst, send_sem=send, recv_sem=recv, device_id=peer, device_id_type=MESH
        )

    def reduce_gather(axis, n, me, others, src, slots, total, s1, r1, s2, r2):
        first = [
            copy(src.at[others[d]], slots.at[d - 1], s1.at[d - 1], r1.at[d - 1], {axis: others[d]})
            for d in range(1, n)
        ]
        for c in first:
            c.start()
        acc = src[me]
        for d in range(1, n):
            first[d - 1].wait_recv()
            acc = acc + slots[d - 1]
        total[me] = acc
        second = [
            copy(total.at[me], total.at[me], s2.at[d - 1], r2.at[d - 1], {axis: others[d]})
            for d in range(1, n)
        ]
        for c in second:
            c.start()
        for d in range(1, n):
            owner = lax.rem(me + n - d, n)
            copy(total.at[owner], total.at[owner], s2.at[d - 1], r2.at[d - 1], {axis: others[d]}).wait_recv()
        for c in first + second:
            c.wait_send()

    reduce_gather("col", nc, ci, cols, part, l_in, left, ls, lr, las, lar)
    total = jnp.zeros((RANK, RANK), F32)
    for k in range(nc):
        block = left[k]
        total += jnp.dot(block.T, block, precision=HIGH, preferred_element_type=F32)
    g_part[...] = total.reshape(g_part.shape)
    reduce_gather("row", nr, ri, rows, g_part, g_in, gram, gs, gr, gas, gar)


def sums(part, nr, nc):
    rows = part.shape[0]
    piece, gpiece = rows // nc, RANK // nr
    vm = pl.BlockSpec(memory_space=VMEM)
    left, gram = pl.pallas_call(
        functools.partial(sums_kernel, nr, nc),
        in_specs=[vm],
        out_specs=[vm, vm],
        out_shape=[
            jax.ShapeDtypeStruct((nc, piece, RANK), F32),
            jax.ShapeDtypeStruct((nr, gpiece, RANK), F32),
        ],
        scratch_shapes=[
            VMEM((nc - 1, piece, RANK), F32),
            VMEM((nr, gpiece, RANK), F32),
            VMEM((nr - 1, gpiece, RANK), F32),
        ]
        + [DMA((nc - 1,))] * 4
        + [DMA((nr - 1,))] * 4,
        compiler_params=pltpu.CompilerParams(
            collective_id=0, has_side_effects=True, vmem_limit_bytes=LIMIT
        ),
    )(part.reshape(nc, piece, RANK))
    return left.reshape(rows, RANK), gram.reshape(RANK, RANK)


def ortho_kernel(gram_ref, left_ref, hi_ref, lo_ref, t_ref, work, inv):
    nb = 32
    gram = gram_ref[...]
    eye = lax.broadcasted_iota(jnp.int32, (RANK, RANK), 0) == lax.broadcasted_iota(
        jnp.int32, (RANK, RANK), 1
    )
    trace = jnp.sum(jnp.sum(jnp.where(eye, gram, 0.0), axis=1, keepdims=True), axis=0, keepdims=True)
    work[:, :RANK] = gram + jnp.where(eye, 1e-06 * trace / RANK, 0.0)
    work[:, RANK:] = eye.astype(F32)
    inv[...] = jnp.zeros_like(inv)
    for r0 in range(0, RANK, nb):
        lo = 0 if r0 < 128 else 128
        width = 384
        panel = work[r0 : r0 + nb, lo : lo + width]
        row_id = lax.broadcasted_iota(jnp.int32, (nb, 1), 0)
        for j in range(nb):
            p = r0 + j - lo
            row = panel[j : j + 1, :]
            factor = panel[:, p : p + 1] / panel[j : j + 1, p : p + 1]
            panel = panel - jnp.where(row_id > j, factor, 0.0) * row
        lane = lax.broadcasted_iota(jnp.int32, (nb, width), 1)
        sub = lax.broadcasted_iota(jnp.int32, (nb, width), 0)
        pivots = jnp.sum(jnp.where(lane == sub + (r0 - lo), panel, 0.0), axis=1, keepdims=True)
        panel = panel / jnp.sqrt(pivots)
        inv[r0 : r0 + nb, 0 : lo + width - RANK] = panel[:, RANK - lo :]
        if r0 + nb < RANK:
            mult = panel[:, : RANK - lo].T
            mult = mult[r0 + nb - lo :, :]
            work[r0 + nb :, lo : lo + width] -= jnp.dot(
                mult, panel, precision=HIGH, preferred_element_type=F32
            )
    ortho = lax.dot_general(
        left_ref[...], inv[...], (((1,), (1,)), ((), ())), precision=HIGH, preferred_element_type=F32
    )
    hi, low = split(ortho)
    hi_ref[...] = hi
    lo_ref[...] = low
    hi, low = split(ortho.T)
    t_ref[:RANK, :] = hi
    t_ref[RANK:, :] = low


def ortho_of(gram, left):
    rows = left.shape[0]
    vm = pl.BlockSpec(memory_space=VMEM)
    return pl.pallas_call(
        ortho_kernel,
        in_specs=[vm, vm],
        out_specs=[vm, vm, vm],
        out_shape=[
            jax.ShapeDtypeStruct((rows, RANK), BF16),
            jax.ShapeDtypeStruct((rows, RANK), BF16),
            jax.ShapeDtypeStruct((2 * RANK, rows), BF16),
        ],
        scratch_shapes=[VMEM((RANK, 2 * RANK), F32), VMEM((RANK, RANK), F32)],
        compiler_params=pltpu.CompilerParams(vmem_limit_bytes=LIMIT),
    )(gram, left)


def right_kernel(g_ref, m_ref, t_ref, out_ref):
    b_hi, b_lo = split(g_ref[...].astype(F32) + m_ref[...].astype(F32))
    both = mm(t_ref[...], b_hi)
    out_ref[...] = both[:RANK] + both[RANK:] + mm(t_ref[:RANK, :], b_lo)


def right_part(g, m, t):
    rows, cols = g.shape
    tile = tile_of(cols)
    return pl.pallas_call(
        right_kernel,
        grid=(cols // tile,),
        in_specs=[
            pl.BlockSpec((rows, tile), lambda i: (0, i)),
            pl.BlockSpec((rows, tile), lambda i: (0, i)),
            whole((2 * RANK, rows)),
        ],
        out_specs=pl.BlockSpec((RANK, tile), lambda i: (0, i)),
        out_shape=jax.ShapeDtypeStruct((RANK, cols), F32),
        compiler_params=pltpu.CompilerParams(vmem_limit_bytes=LIMIT),
    )(g, m, t)


def total_kernel(nr, nc, x, out, sq, c_in, l_in, r_in, acc, sqs, cs, cr, rs, lr, rr, fl, fr, fz, ps, pr, ss, sr):
    nz = nr // 2
    half = x.shape[0] // 2
    ri, ci = lax.axis_index("row"), lax.axis_index("col")
    z, core = ri // 2, lax.rem(ri, 2)
    partner = ri + 1 - 2 * core
    mine, theirs = core * half, (1 - core) * half
    lower, upper = jnp.maximum(ri - 2, core), jnp.minimum(ri + 2, nr - 2 + core)
    cols = [lax.rem(ci + d, nc) for d in range(nc)]
    has_l, has_r = z > 0, z < nz - 1

    barrier = greet([{"row": partner}] + [{"col": p} for p in cols[1:]])

    @pl.when(has_l)
    def _():
        pl.semaphore_signal(barrier, inc=1, device_id={"row": lower}, device_id_type=MESH)

    @pl.when(has_r)
    def _():
        pl.semaphore_signal(barrier, inc=1, device_id={"row": upper}, device_id_type=MESH)

    pl.semaphore_wait(barrier, nc + jnp.minimum(z, 1) + jnp.minimum(nz - 1 - z, 1))

    def copy(src, dst, send, recv, peer, axis="row"):
        return pltpu.make_async_remote_copy(
            src_ref=src, dst_ref=dst, send_sem=send, recv_sem=recv, device_id={axis: peer}, device_id_type=MESH
        )

    def core_copy(s):
        return copy(x.at[theirs + s], c_in.at[s], cs.at[s], cr.at[s], partner)

    def up(s):
        return copy(acc.at[s], l_in.at[s], rs.at[s], lr.at[s], upper)

    def down(s):
        return copy(acc.at[s], r_in.at[s], rs.at[s], rr.at[s], lower)

    def final_down(s):
        return copy(out.at[mine + s], out.at[mine + s], fl.at[s], fz.at[s], lower)

    def final_up(s):
        return copy(out.at[mine + s], out.at[mine + s], fr.at[s], fz.at[s], upper)

    def share(s):
        return copy(out.at[mine + s], out.at[mine + s], ps.at[s], pr.at[s], partner)

    def share_in(s):
        return copy(out.at[theirs + s], out.at[theirs + s], ps.at[s], pr.at[s], partner)

    def centre(s):
        return nz // 2 - 1 + lax.rem(s, 2)

    def from_lower(s):
        @pl.when(has_l)
        def _():
            up(s).wait_recv()
            acc[s] += l_in[s]

    def from_upper(s):
        @pl.when(has_r)
        def _():
            down(s).wait_recv()
            acc[s] += r_in[s]

    def reduce(s):
        mid = centre(s)
        core_copy(s).wait_recv()
        acc[s] = x[mine + s] + c_in[s]

        @pl.when(z < mid)
        def _():
            from_lower(s)
            up(s).start()

        @pl.when(z > mid)
        def _():
            from_upper(s)
            down(s).start()

        @pl.when(z == mid)
        def _():
            from_lower(s)
            from_upper(s)
            out[mine + s] = acc[s]

            @pl.when(has_l)
            def _():
                final_down(s).start()

            @pl.when(has_r)
            def _():
                final_up(s).start()

            share(s).start()

    def spread(s):
        mid = centre(s)

        @pl.when(z < mid)
        def _():
            final_down(s).wait_recv()

            @pl.when(has_l)
            def _():
                final_down(s).start()

            share(s).start()

        @pl.when(z > mid)
        def _():
            final_up(s).wait_recv()

            @pl.when(has_r)
            def _():
                final_up(s).start()

            share(s).start()

    def loop(lo, hi, body):
        def step(s, carry):
            body(s)
            return carry

        lax.fori_loop(lo, hi, step, 0)

    loop(0, half, lambda s: core_copy(s).start())

    end = jnp.logical_or(z == 0, z == nz - 1)

    if nz > 2:

        @pl.when(end)
        def _():
            loop(0, half, reduce)
            loop(0, half, spread)

        @pl.when(jnp.logical_not(end))
        def _():
            loop(0, 2, reduce)

            def both(t):
                reduce(t)
                spread(t - 2)

            loop(2, half, both)
            loop(half - 2, half, spread)

    else:
        loop(0, half, reduce)
        loop(0, half, spread)

    lane = lax.broadcasted_iota(jnp.int32, (8, 128), 1)

    def square(i, carry):
        v = out[i]
        return carry + jnp.where(lane == i, jnp.sum(v * v, axis=1, keepdims=True), 0.0)

    def own(s, carry):
        return square(mine + s, carry)

    def other(s, carry):
        share_in(s).wait_recv()
        return square(theirs + s, carry)

    carry = lax.fori_loop(0, half, own, jnp.zeros((8, 128), F32))
    sqs[0] = lax.fori_loop(0, half, other, carry)
    sends = [copy(sqs.at[0], sqs.at[d], ss.at[d - 1], sr.at[d - 1], cols[d], "col") for d in range(1, nc)]
    for c in sends:
        c.start()

    def drain(s):
        mid = centre(s)
        core_copy(s).wait_send()

        @pl.when(z != mid)
        def _():
            up(s).wait_send()

        @pl.when(jnp.logical_and(z <= mid, has_l))
        def _():
            final_down(s).wait_send()

        @pl.when(jnp.logical_and(z >= mid, has_r))
        def _():
            final_up(s).wait_send()

        share(s).wait_send()

    loop(0, half, drain)
    total = sqs[0]
    for d in range(1, nc):
        sends[d - 1].wait_recv()
        total = total + sqs[d]
    for c in sends:
        c.wait_send()
    for i in range(2 * half):
        sq[i] = jnp.broadcast_to(total[:, i : i + 1], (8, 128))


def right_total(part, nr, nc):
    cols = part.shape[1]
    n = RANK // 8
    half = n // 2
    vm = pl.BlockSpec(memory_space=VMEM)
    piece = VMEM((half, 8, cols), F32)
    out, sq = pl.pallas_call(
        functools.partial(total_kernel, nr, nc),
        in_specs=[vm],
        out_specs=[vm, vm],
        out_shape=[
            jax.ShapeDtypeStruct((n, 8, cols), F32),
            jax.ShapeDtypeStruct((n, 8, 128), F32),
        ],
        scratch_shapes=[piece, piece, piece, piece, VMEM((nc, 8, 128), F32)]
        + [DMA((half,))] * 10
        + [DMA((nc - 1,))] * 2,
        compiler_params=pltpu.CompilerParams(
            collective_id=1, has_side_effects=True, vmem_limit_bytes=LIMIT
        ),
    )(part.reshape(n, 8, cols))
    return out.reshape(RANK, cols), sq.reshape(RANK, 128)


def final_kernel(scale, g_ref, m_ref, w_ref, hi_ref, lo_ref, rt_ref, sq_ref, nw_ref, nm_ref, nf_ref):
    rt = rt_ref[...]
    hi = hi_ref[...]
    ft = rt / jnp.sqrt(sq_ref[:, :1] / COLS + 1e-06)
    nf_ref[...] = ft.T
    buffer = g_ref[...].astype(F32) + m_ref[...].astype(F32)
    nm_ref[...] = (buffer - (1.0 - decay) * mm(hi, rt.astype(BF16))).astype(BF16)
    f_hi, f_lo = split(ft)
    update = mm(hi, f_hi) + mm(lo_ref[...], f_hi) + mm(hi, f_lo)
    nw_ref[...] = (w_ref[...].astype(F32) - scale * update).astype(BF16)


def final(g, m, w, hi, lo, rt, sq):
    rows, cols = g.shape
    tile = tile_of(cols)
    block = pl.BlockSpec((rows, tile), lambda i: (0, i))
    return pl.pallas_call(
        functools.partial(final_kernel, step_size * (ROWS / RANK) ** 0.5),
        grid=(cols // tile,),
        in_specs=[
            block,
            block,
            block,
            whole((rows, RANK)),
            whole((rows, RANK)),
            pl.BlockSpec((RANK, tile), lambda i: (0, i)),
            whole((RANK, 128)),
        ],
        out_specs=[block, block, pl.BlockSpec((tile, RANK), lambda i: (i, 0))],
        out_shape=[
            jax.ShapeDtypeStruct((rows, cols), BF16),
            jax.ShapeDtypeStruct((rows, cols), BF16),
            jax.ShapeDtypeStruct((cols, RANK), F32),
        ],
        compiler_params=pltpu.CompilerParams(vmem_limit_bytes=LIMIT),
    )(g, m, w, hi, lo, rt, sq)


def local(nr, nc, gradient, momentum, weight, right_factor):
    part = left_part(gradient, momentum, right_factor)
    left, gram = sums(part, nr, nc)
    hi, lo, t = ortho_of(gram, left)
    rt, sq = right_total(right_part(gradient, momentum, t), nr, nc)
    return tuple(final(gradient, momentum, weight, hi, lo, rt, sq))


def solution(mesh):
    in_specs = (P("row", "col"), P("row", "col"), P("row", "col"), P("col", None))
    out_specs = (P("row", "col"), P("row", "col"), P("col", None))
    body = functools.partial(local, mesh.shape["row"], mesh.shape["col"])
    return jax.shard_map(body, mesh=mesh, in_specs=in_specs, out_specs=out_specs, check_vma=False)
```

time: 546 us -> 317 us (0.58)
  Pallas kernels: 0 us -> 316 us
  waiting for transfers between devices: 255 us -> 0 us
  matrix products: 188 us -> 0 us
  other arithmetic: 64.6 us -> 0 us
  between operations: 16.1 us -> 0.65 us
  blocking collectives: 10 us -> 0 us
  local copies, waits for them, and re-layouts: 5.5 us -> 0 us
    pallas_call x0 -> x6, Pallas kernels: none -> 316 us  [the longest x1 165 us: right_total(): pl.pallas_call(functools.partial(total_kernel, nr, nc), in_specs=[vm], ou...]
    psum x3 -> x0, waiting for transfers between devices: 255 us -> none  [the longest x1 145 us: local(): right_part = lax.psum(cross_product(buffer, ortho), 'row')]
    dot_general x5 -> x0, matrix products: 183 us -> none  [the longest x1 52.2 us: local(): jnp.dot(ortho, right_part.T, precision=high)]
    another operation x9 -> x0, other arithmetic: 53.7 us -> none  [the longest x6 34 us: factor_gram(): return jnp.linalg.cholesky(gram + jitter * jnp.eye(rank, dtype=jnp.float32))]
    psum x1 -> x0, blocking collectives: 10 us -> none  [local(): squares = lax.psum(jnp.sum(right_part * right_part, axis=0), 'col')]
  transfers between devices with their start and end apart: 3 -> 0, of which waited for: 3 -> 0; matrix products, arithmetic and copies ran while one was open for 0% -> 0% of each run, Pallas kernels for 0% -> 0%
where the time goes in v1:
time: 317 us; the launch traced here: 316 us
  Pallas kernels  316 us (100%)
    pallas_call x1, Pallas kernels, right_total(): pl.pallas_call(functools.partial(total_kernel, nr, nc), in_specs=[vm], ou...  165 us
    pallas_call x1, Pallas kernels, sums(): pl.pallas_call(functools.partial(sums_kernel, nr, nc), in_specs=[vm], out...  47.1 us
    pallas_call x1, Pallas kernels, final(): pl.pallas_call(functools.partial(final_kernel, step_size * (ROWS / RANK)...  34.1 us
    pallas_call x1, Pallas kernels, ortho_of(): pl.pallas_call(ortho_kernel, in_specs=[vm, vm], out_specs=[vm, vm, vm], o...  27.6 us
    pallas_call x1, Pallas kernels, right_part(): pl.pallas_call(right_kernel, grid=(cols // tile,), in_specs=[pl.BlockSpec...  20.8 us
    pallas_call x1, Pallas kernels, left_part(): pl.pallas_call(left_kernel, grid=(cols // tile,), in_specs=[pl.BlockSpec(...  20.6 us

profile of v1, /device:TPU:0, one launch (start us, length us, event | category | flops | bytes accessed | tf_op | source)
XLA Modules:
  0.0 316.3 jit_solution(12666659943177688293)
XLA Ops:
  0.6 20.6 %shard_map.67 = f32[1024,256]{1,0:T(8,128)} custom-call(bf16[1024,6656]{1,0:T(8,128)(2,1)} %g_ref.5, bf16[1024,6656]{1,0:T(8,128)(2,1)} %m_ref.5, f32[6656,256]{1,0:T(8,128)} %r_ref.1), custom_call_target="tpu_custom_call" | custom-call | tf_op jit(solution)/shard_map/pallas_call | solution.py:59
  21.3 47.1 %shard_map.68 = (f32[4,256,256]{2,1,0:T(8,128)}, f32[8,32,256]{2,1,0:T(8,128)}) custom-call(f32[4,256,256]{2,1,0:T(8,128)} %bitcast.8), custom_call_target="tpu_custom_call" | custom-call | tf_op jit(solution)/shard_map/pallas_call | solution.py:129
  68.4 27.6 %shard_map.69 = (bf16[1024,256]{1,0:T(8,128)(2,1)}, bf16[1024,256]{1,0:T(8,128)(2,1)}, bf16[512,1024]{1,0:T(8,128)(2,1)}) custom-call(f32[256,256]{1,0:T(8,128)} %bitcast.10, f32[1024,256]{1,0:T(8,128)} %bitcast.9), custom_call_target="tpu_custom_call" | custom-call | tf_op jit(solution)/shard_map/pallas_call | solution.py:196
  96.0 20.8 %shard_map.70 = f32[256,6656]{1,0:T(8,128)} custom-call(bf16[1024,6656]{1,0:T(8,128)(2,1)} %g_ref.5, bf16[1024,6656]{1,0:T(8,128)(2,1)} %m_ref.5, bf16[512,1024]{1,0:T(8,128)(2,1)} %get-tuple-element.14.t_ref), custom_call_target="tpu_custom_call" | custom-call | tf_op jit(solution)/shard_map/pallas_call | solution.py:219
  116.8 165.4 %shard_map.71 = (f32[32,8,6656]{2,1,0:T(8,128)}, f32[32,8,128]{2,1,0:T(8,128)}) custom-call(f32[32,8,6656]{2,1,0:T(8,128)} %bitcast.6), custom_call_target="tpu_custom_call" | custom-call | tf_op jit(solution)/shard_map/pallas_call | solution.py:438
  282.3 34.1 %shard_map.72 = (bf16[1024,6656]{1,0:T(8,128)(2,1)}, bf16[1024,6656]{1,0:T(8,128)(2,1)}, f32[6656,256]{1,0:T(8,128)}) custom-call(bf16[1024,6656]{1,0:T(8,128)(2,1)} %g_ref.5, bf16[1024,6656]{1,0:T(8,128)(2,1)} %m_ref.5, bf16[1024,6656]{1,0:T(8,128)(2,1)} %w_ref.1, bf16[1024,256]{1,0:T(8,128)(2,1)} %get-tuple-element.12.hi_ref, ...), custom_call_target="tpu_custom_call" | custom-call | tf_op jit(solution)/shard_map/pallas_call | solution.py:472

commit v2 on v1

--- a/solution.py
+++ b/solution.py
@@ -48,9 +48,9 @@
     def _():
         out_ref[...] = jnp.zeros_like(out_ref)
 
-    b_hi, b_lo = split(g_ref[...].astype(F32) + m_ref[...].astype(F32))
+    g, m = g_ref[...], m_ref[...]
     r_hi, r_lo = split(r_ref[...])
-    out_ref[...] += mm(b_hi, r_hi) + mm(b_lo, r_hi) + mm(b_hi, r_lo)
+    out_ref[...] += mm(jnp.concatenate([g, m, g, m], axis=1), jnp.concatenate([r_hi, r_hi, r_lo, r_lo], axis=0))
 
 
 def left_part(g, m, r):
@@ -148,8 +148,8 @@
     return left.reshape(rows, RANK), gram.reshape(RANK, RANK)
 
 
-def ortho_kernel(gram_ref, left_ref, hi_ref, lo_ref, t_ref, work, inv):
-    nb = 32
+def ortho_kernel(gram_ref, left_ref, o_ref, t_ref, work, inv):
+    nb, group = 32, 8
     gram = gram_ref[...]
     eye = lax.broadcasted_iota(jnp.int32, (RANK, RANK), 0) == lax.broadcasted_iota(
         jnp.int32, (RANK, RANK), 1
@@ -162,12 +162,19 @@
         lo = 0 if r0 < 128 else 128
         width = 384
         panel = work[r0 : r0 + nb, lo : lo + width]
-        row_id = lax.broadcasted_iota(jnp.int32, (nb, 1), 0)
-        for j in range(nb):
-            p = r0 + j - lo
-            row = panel[j : j + 1, :]
-            factor = panel[:, p : p + 1] / panel[j : j + 1, p : p + 1]
-            panel = panel - jnp.where(row_id > j, factor, 0.0) * row
+        row_id = lax.broadcasted_iota(jnp.int32, (nb, 128), 0)
+        for j0 in range(0, nb, group):
+            p = r0 + j0 - lo
+            column = [
+                jnp.broadcast_to(panel[:, p + k : p + k + 1], (nb, 128)) for k in range(group)
+            ]
+            for k in range(group):
+                j = j0 + k
+                factor = column[k] * (1.0 / column[k][j : j + 1, :])
+                factor = jnp.where(row_id > j, factor, 0.0)
+                for q in range(k + 1, group):
+                    column[q] = column[q] - factor * column[q][j : j + 1, :]
+                panel = panel - jnp.concatenate([factor] * (width // 128), axis=1) * panel[j : j + 1, :]
         lane = lax.broadcasted_iota(jnp.int32, (nb, width), 1)
         sub = lax.broadcasted_iota(jnp.int32, (nb, width), 0)
         pivots = jnp.sum(jnp.where(lane == sub + (r0 - lo), panel, 0.0), axis=1, keepdims=True)
@@ -183,8 +190,7 @@
         left_ref[...], inv[...], (((1,), (1,)), ((), ())), precision=HIGH, preferred_element_type=F32
     )
     hi, low = split(ortho)
-    hi_ref[...] = hi
-    lo_ref[...] = low
+    o_ref[...] = jnp.concatenate([hi, low, hi], axis=1)
     hi, low = split(ortho.T)
     t_ref[:RANK, :] = hi
     t_ref[RANK:, :] = low
@@ -196,10 +202,9 @@
     return pl.pallas_call(
         ortho_kernel,
         in_specs=[vm, vm],
-        out_specs=[vm, vm, vm],
+        out_specs=[vm, vm],
         out_shape=[
-            jax.ShapeDtypeStruct((rows, RANK), BF16),
-            jax.ShapeDtypeStruct((rows, RANK), BF16),
+            jax.ShapeDtypeStruct((rows, 3 * RANK), BF16),
             jax.ShapeDtypeStruct((2 * RANK, rows), BF16),
         ],
         scratch_shapes=[VMEM((RANK, 2 * RANK), F32), VMEM((RANK, RANK), F32)],
@@ -208,9 +213,9 @@
 
 
 def right_kernel(g_ref, m_ref, t_ref, out_ref):
-    b_hi, b_lo = split(g_ref[...].astype(F32) + m_ref[...].astype(F32))
-    both = mm(t_ref[...], b_hi)
-    out_ref[...] = both[:RANK] + both[RANK:] + mm(t_ref[:RANK, :], b_lo)
+    t = t_ref[...]
+    both = mm(jnp.concatenate([t, t], axis=1), jnp.concatenate([g_ref[...], m_ref[...]], axis=0))
+    out_ref[...] = both[:RANK] + both[RANK:]
 
 
 def right_part(g, m, t):
@@ -280,7 +285,7 @@
         return copy(out.at[theirs + s], out.at[theirs + s], ps.at[s], pr.at[s], partner)
 
     def centre(s):
-        return nz // 2 - 1 + lax.rem(s, 2)
+        return nz // 2 - 1 + lax.rem(s + core, 2)
 
     def from_lower(s):
         @pl.when(has_l)
@@ -453,19 +458,18 @@
     return out.reshape(RANK, cols), sq.reshape(RANK, 128)
 
 
-def final_kernel(scale, g_ref, m_ref, w_ref, hi_ref, lo_ref, rt_ref, sq_ref, nw_ref, nm_ref, nf_ref):
+def final_kernel(scale, g_ref, m_ref, w_ref, o_ref, rt_ref, sq_ref, nw_ref, nm_ref, nf_ref):
     rt = rt_ref[...]
-    hi = hi_ref[...]
     ft = rt / jnp.sqrt(sq_ref[:, :1] / COLS + 1e-06)
     nf_ref[...] = ft.T
     buffer = g_ref[...].astype(F32) + m_ref[...].astype(F32)
-    nm_ref[...] = (buffer - (1.0 - decay) * mm(hi, rt.astype(BF16))).astype(BF16)
-    f_hi, f_lo = split(ft)
-    update = mm(hi, f_hi) + mm(lo_ref[...], f_hi) + mm(hi, f_lo)
-    nw_ref[...] = (w_ref[...].astype(F32) - scale * update).astype(BF16)
-
-
-def final(g, m, w, hi, lo, rt, sq):
+    nm_ref[...] = (buffer - mm(o_ref[:, :RANK], ((1.0 - decay) * rt).astype(BF16))).astype(BF16)
+    f_hi, f_lo = split(scale * ft)
+    update = mm(o_ref[...], jnp.concatenate([f_hi, f_hi, f_lo], axis=0))
+    nw_ref[...] = (w_ref[...].astype(F32) - update).astype(BF16)
+
+
+def final(g, m, w, o, rt, sq):
     rows, cols = g.shape
     tile = tile_of(cols)
     block = pl.BlockSpec((rows, tile), lambda i: (0, i))
@@ -476,8 +480,7 @@
             block,
             block,
             block,
-            whole((rows, RANK)),
-            whole((rows, RANK)),
+            whole((rows, 3 * RANK)),
             pl.BlockSpec((RANK, tile), lambda i: (0, i)),
             whole((RANK, 128)),
         ],
@@ -488,15 +491,15 @@
             jax.ShapeDtypeStruct((cols, RANK), F32),
         ],
         compiler_params=pltpu.CompilerParams(vmem_limit_bytes=LIMIT),
-    )(g, m, w, hi, lo, rt, sq)
+    )(g, m, w, o, rt, sq)
 
 
 def local(nr, nc, gradient, momentum, weight, right_factor):
     part = left_part(gradient, momentum, right_factor)
     left, gram = sums(part, nr, nc)
-    hi, lo, t = ortho_of(gram, left)
+    o, t = ortho_of(gram, left)
     rt, sq = right_total(right_part(gradient, momentum, t), nr, nc)
-    return tuple(final(gradient, momentum, weight, hi, lo, rt, sq))
+    return tuple(final(gradient, momentum, weight, o, rt, sq))
 
 
 def solution(mesh):

time: 317 us -> 324 us (1.022)
  Pallas kernels: 316 us -> 323 us
    pallas_call x1, Pallas kernels: 165 us -> 184 us  [right_total(): pl.pallas_call(functools.partial(total_kernel, nr, nc), in_specs=[vm], ou...]
    pallas_call x1, Pallas kernels: 27.6 us -> 13.6 us  [ortho_of(): pl.pallas_call(ortho_kernel, in_specs=[vm, vm], out_specs=[vm, vm], out_s...]
where the time goes in v2:
time: 324 us; the launch traced here: 323 us
  Pallas kernels  323 us (100%)
    pallas_call x1, Pallas kernels, right_total(): pl.pallas_call(functools.partial(total_kernel, nr, nc), in_specs=[vm], ou...  184 us
    pallas_call x1, Pallas kernels, sums(): pl.pallas_call(functools.partial(sums_kernel, nr, nc), in_specs=[vm], out...  47.1 us
    pallas_call x1, Pallas kernels, final(): pl.pallas_call(functools.partial(final_kernel, step_size * (ROWS / RANK)...  34.2 us
    pallas_call x1, Pallas kernels, right_part(): pl.pallas_call(right_kernel, grid=(cols // tile,), in_specs=[pl.BlockSpec...  22.2 us
    pallas_call x1, Pallas kernels, left_part(): pl.pallas_call(left_kernel, grid=(cols // tile,), in_specs=[pl.BlockSpec(...  22 us
    pallas_call x1, Pallas kernels, ortho_of(): pl.pallas_call(ortho_kernel, in_specs=[vm, vm], out_specs=[vm, vm], out_s...  13.6 us

profile of v2, /device:TPU:0, one launch (start us, length us, event | category | flops | bytes accessed | tf_op | source)
XLA Modules:
  0.0 323.4 jit_solution(16267165095367581155)
XLA Ops:
  0.6 22.0 %shard_map.67 = f32[1024,256]{1,0:T(8,128)} custom-call(bf16[1024,6656]{1,0:T(8,128)(2,1)} %g_ref.5, bf16[1024,6656]{1,0:T(8,128)(2,1)} %m_ref.5, f32[6656,256]{1,0:T(8,128)} %r_ref.1), custom_call_target="tpu_custom_call" | custom-call | tf_op jit(solution)/shard_map/pallas_call | solution.py:59
  22.6 47.1 %shard_map.68 = (f32[4,256,256]{2,1,0:T(8,128)}, f32[8,32,256]{2,1,0:T(8,128)}) custom-call(f32[4,256,256]{2,1,0:T(8,128)} %bitcast.8), custom_call_target="tpu_custom_call" | custom-call | tf_op jit(solution)/shard_map/pallas_call | solution.py:129
  69.7 13.6 %shard_map.69 = (bf16[1024,768]{1,0:T(8,128)(2,1)}, bf16[512,1024]{1,0:T(8,128)(2,1)}) custom-call(f32[256,256]{1,0:T(8,128)} %bitcast.10, f32[1024,256]{1,0:T(8,128)} %bitcast.9), custom_call_target="tpu_custom_call" | custom-call | tf_op jit(solution)/shard_map/pallas_call | solution.py:202
  83.4 22.2 %shard_map.70 = f32[256,6656]{1,0:T(8,128)} custom-call(bf16[1024,6656]{1,0:T(8,128)(2,1)} %g_ref.5, bf16[1024,6656]{1,0:T(8,128)(2,1)} %m_ref.5, bf16[512,1024]{1,0:T(8,128)(2,1)} %get-tuple-element.12.t_ref), custom_call_target="tpu_custom_call" | custom-call | tf_op jit(solution)/shard_map/pallas_call | solution.py:224
  105.6 183.6 %shard_map.71 = (f32[32,8,6656]{2,1,0:T(8,128)}, f32[32,8,128]{2,1,0:T(8,128)}) custom-call(f32[32,8,6656]{2,1,0:T(8,128)} %bitcast.6), custom_call_target="tpu_custom_call" | custom-call | tf_op jit(solution)/shard_map/pallas_call | solution.py:443
  289.1 34.2 %shard_map.72 = (bf16[1024,6656]{1,0:T(8,128)(2,1)}, bf16[1024,6656]{1,0:T(8,128)(2,1)}, f32[6656,256]{1,0:T(8,128)}) custom-call(bf16[1024,6656]{1,0:T(8,128)(2,1)} %g_ref.5, bf16[1024,6656]{1,0:T(8,128)(2,1)} %m_ref.5, bf16[1024,6656]{1,0:T(8,128)(2,1)} %w_ref.1, bf16[1024,768]{1,0:T(8,128)(2,1)} %get-tuple-element.11.o_ref, f32[256,6656]{1,0:T(8,128)} %bitcast.7, ...), custom_call_target="tpu_custom_call" | custom-call | tf_op jit(solution)/shard_map/pallas_call | solution.py:476

commit v3 on v2

--- a/solution.py
+++ b/solution.py
@@ -212,39 +212,28 @@
     )(gram, left)
 
 
-def right_kernel(g_ref, m_ref, t_ref, out_ref):
-    t = t_ref[...]
-    both = mm(jnp.concatenate([t, t], axis=1), jnp.concatenate([g_ref[...], m_ref[...]], axis=0))
-    out_ref[...] = both[:RANK] + both[RANK:]
-
-
-def right_part(g, m, t):
-    rows, cols = g.shape
-    tile = tile_of(cols)
-    return pl.pallas_call(
-        right_kernel,
-        grid=(cols // tile,),
-        in_specs=[
-            pl.BlockSpec((rows, tile), lambda i: (0, i)),
-            pl.BlockSpec((rows, tile), lambda i: (0, i)),
-            whole((2 * RANK, rows)),
-        ],
-        out_specs=pl.BlockSpec((RANK, tile), lambda i: (0, i)),
-        out_shape=jax.ShapeDtypeStruct((RANK, cols), F32),
-        compiler_params=pltpu.CompilerParams(vmem_limit_bytes=LIMIT),
-    )(g, m, t)
-
-
-def total_kernel(nr, nc, x, out, sq, c_in, l_in, r_in, acc, sqs, cs, cr, rs, lr, rr, fl, fr, fz, ps, pr, ss, sr):
+def right_kernel(nr, nc, g, m, t_ref, out, sq, g_buf, m_buf, x, c_in, l_in, r_in, acc, sqs, gs, ms, cs, cr, rs, lr, rr, fl, fr, fz, ps, pr, ss, sr):
     nz = nr // 2
-    half = x.shape[0] // 2
+    n, tile = x.shape[0], x.shape[3]
     ri, ci = lax.axis_index("row"), lax.axis_index("col")
     z, core = ri // 2, lax.rem(ri, 2)
+    other = 1 - core
     partner = ri + 1 - 2 * core
-    mine, theirs = core * half, (1 - core) * half
     lower, upper = jnp.maximum(ri - 2, core), jnp.minimum(ri + 2, nr - 2 + core)
     cols = [lax.rem(ci + d, nc) for d in range(nc)]
     has_l, has_r = z > 0, z < nz - 1
+
+    def fetch(s):
+        at = pl.ds(pl.multiple_of(s * tile, tile), tile)
+        slot = lax.rem(s, 2)
+        return (
+            pltpu.make_async_copy(g.at[:, at], g_buf.at[slot], gs.at[slot]),
+            pltpu.make_async_copy(m.at[:, at], m_buf.at[slot], ms.at[slot]),
+        )
+
+    for s in range(min(2, n)):
+        for c in fetch(s):
+            c.start()
 
     barrier = greet([{"row": partner}] + [{"col": p} for p in cols[1:]])
 
@@ -264,7 +253,7 @@
         )
 
     def core_copy(s):
-        return copy(x.at[theirs + s], c_in.at[s], cs.at[s], cr.at[s], partner)
+        return copy(x.at[s, other], c_in.at[s], cs.at[s], cr.at[s], partner)
 
     def up(s):
         return copy(acc.at[s], l_in.at[s], rs.at[s], lr.at[s], upper)
@@ -273,20 +262,34 @@
         return copy(acc.at[s], r_in.at[s], rs.at[s], rr.at[s], lower)
 
     def final_down(s):
-        return copy(out.at[mine + s], out.at[mine + s], fl.at[s], fz.at[s], lower)
+        return copy(out.at[s, core], out.at[s, core], fl.at[s], fz.at[s], lower)
 
     def final_up(s):
-        return copy(out.at[mine + s], out.at[mine + s], fr.at[s], fz.at[s], upper)
+        return copy(out.at[s, core], out.at[s, core], fr.at[s], fz.at[s], upper)
 
     def share(s):
-        return copy(out.at[mine + s], out.at[mine + s], ps.at[s], pr.at[s], partner)
+        return copy(out.at[s, core], out.at[s, core], ps.at[s], pr.at[s], partner)
 
     def share_in(s):
-        return copy(out.at[theirs + s], out.at[theirs + s], ps.at[s], pr.at[s], partner)
+        return copy(out.at[s, other], out.at[s, other], ps.at[s], pr.at[s], partner)
 
     def centre(s):
         return nz // 2 - 1 + lax.rem(s + core, 2)
 
+    def product(s):
+        slot = lax.rem(s, 2)
+        for c in fetch(s):
+            c.wait()
+        t = t_ref[...]
+        both = mm(jnp.concatenate([t, t], axis=1), jnp.concatenate([g_buf[slot], m_buf[slot]], axis=0))
+        x[s] = (both[:RANK] + both[RANK:]).reshape(2, RANK // 2, tile)
+        core_copy(s).start()
+
+        @pl.when(s + 2 < n)
+        def _():
+            for c in fetch(s + 2):
+                c.start()
+
     def from_lower(s):
         @pl.when(has_l)
         def _():
@@ -299,10 +302,10 @@
             down(s).wait_recv()
             acc[s] += r_in[s]
 
-    def reduce(s):
+    def forward(s):
         mid = centre(s)
         core_copy(s).wait_recv()
-        acc[s] = x[mine + s] + c_in[s]
+        acc[s] = x[s, core] + c_in[s]
 
         @pl.when(z < mid)
         def _():
@@ -314,11 +317,12 @@
             from_upper(s)
             down(s).start()
 
-        @pl.when(z == mid)
+    def total(s):
+        @pl.when(z == centre(s))
         def _():
             from_lower(s)
             from_upper(s)
-            out[mine + s] = acc[s]
+            out[s, core] = acc[s]
 
             @pl.when(has_l)
             def _():
@@ -360,107 +364,111 @@
 
         lax.fori_loop(lo, hi, step, 0)
 
-    loop(0, half, lambda s: core_copy(s).start())
-
-    end = jnp.logical_or(z == 0, z == nz - 1)
+    def stages(lags):
+        def body(i):
+            for work, lag in lags:
+
+                @pl.when(jnp.logical_and(i >= lag, i < n + lag))
+                def _():
+                    work(i - lag)
+
+        loop(0, n + max(lag for _, lag in lags), body)
 
     if nz > 2:
+        end = jnp.logical_or(z == 0, z == nz - 1)
 
         @pl.when(end)
         def _():
-            loop(0, half, reduce)
-            loop(0, half, spread)
+            stages([(product, 0), (forward, 2)])
+            loop(0, n, spread)
 
         @pl.when(jnp.logical_not(end))
         def _():
-            loop(0, 2, reduce)
-
-            def both(t):
-                reduce(t)
-                spread(t - 2)
-
-            loop(2, half, both)
-            loop(half - 2, half, spread)
+            stages([(product, 0), (forward, 2), (total, 4), (spread, 6)])
 
     else:
-        loop(0, half, reduce)
-        loop(0, half, spread)
-
-    lane = lax.broadcasted_iota(jnp.int32, (8, 128), 1)
-
-    def square(i, carry):
-        v = out[i]
-        return carry + jnp.where(lane == i, jnp.sum(v * v, axis=1, keepdims=True), 0.0)
-
-    def own(s, carry):
-        return square(mine + s, carry)
-
-    def other(s, carry):
+        stages([(product, 0), (forward, 2), (total, 4), (spread, 6)])
+
+    def drain(s):
+        mid = centre(s)
+        core_copy(s).wait_send()
+
+        @pl.when(z != mid)
+        def _():
+            up(s).wait_send()
+
+        @pl.when(jnp.logical_and(z <= mid, has_l))
+        def _():
+            final_down(s).wait_send()
+
+        @pl.when(jnp.logical_and(z >= mid, has_r))
+        def _():
+            final_up(s).wait_send()
+
+        share(s).wait_send()
         share_in(s).wait_recv()
-        return square(theirs + s, carry)
-
-    carry = lax.fori_loop(0, half, own, jnp.zeros((8, 128), F32))
-    sqs[0] = lax.fori_loop(0, half, other, carry)
+
+    loop(0, n, drain)
+
+    def square(s, carry):
+        v = out[s].reshape(RANK, tile)
+        for k in range(tile // 128):
+            w = v[:, k * 128 : (k + 1) * 128]
+            carry = carry + w * w
+        return carry
+
+    squares = lax.fori_loop(0, n, square, jnp.zeros((RANK, 128), F32))
+    sqs[0] = jnp.broadcast_to(jnp.sum(squares.T, axis=0, keepdims=True), (8, RANK))
     sends = [copy(sqs.at[0], sqs.at[d], ss.at[d - 1], sr.at[d - 1], cols[d], "col") for d in range(1, nc)]
     for c in sends:
         c.start()
-
-    def drain(s):
-        mid = centre(s)
-        core_copy(s).wait_send()
-
-        @pl.when(z != mid)
-        def _():
-            up(s).wait_send()
-
-        @pl.when(jnp.logical_and(z <= mid, has_l))
-        def _():
-            final_down(s).wait_send()
-
-        @pl.when(jnp.logical_and(z >= mid, has_r))
-        def _():
-            final_up(s).wait_send()
-
-        share(s).wait_send()
-
-    loop(0, half, drain)
-    total = sqs[0]
+    total_sq = sqs[0]
     for d in range(1, nc):
         sends[d - 1].wait_recv()
-        total = total + sqs[d]
+        total_sq = total_sq + sqs[d]
     for c in sends:
         c.wait_send()
-    for i in range(2 * half):
-        sq[i] = jnp.broadcast_to(total[:, i : i + 1], (8, 128))
-
-
-def right_total(part, nr, nc):
-    cols = part.shape[1]
-    n = RANK // 8
-    half = n // 2
+    sq[...] = total_sq
+
+
+def right_total(g, m, t, nr, nc):
+    rows, cols = g.shape
+    tile = min(tile_of(cols), 256)
+    n = cols // tile
     vm = pl.BlockSpec(memory_space=VMEM)
-    piece = VMEM((half, 8, cols), F32)
+    hbm = pl.BlockSpec(memory_space=pl.ANY)
+    piece = VMEM((n, RANK // 2, tile), F32)
     out, sq = pl.pallas_call(
-        functools.partial(total_kernel, nr, nc),
-        in_specs=[vm],
+        functools.partial(right_kernel, nr, nc),
+        in_specs=[hbm, hbm, vm],
         out_specs=[vm, vm],
         out_shape=[
-            jax.ShapeDtypeStruct((n, 8, cols), F32),
-            jax.ShapeDtypeStruct((n, 8, 128), F32),
+            jax.ShapeDtypeStruct((n, 2, RANK // 2, tile), F32),
+            jax.ShapeDtypeStruct((8, RANK), F32),
         ],
-        scratch_shapes=[piece, piece, piece, piece, VMEM((nc, 8, 128), F32)]
-        + [DMA((half,))] * 10
+        scratch_shapes=[
+            VMEM((2, rows, tile), BF16),
+            VMEM((2, rows, tile), BF16),
+            VMEM((n, 2, RANK // 2, tile), F32),
+            piece,
+            piece,
+            piece,
+            piece,
+            VMEM((nc, 8, RANK), F32),
+        ]
+        + [DMA((2,))] * 2
+        + [DMA((n,))] * 10
         + [DMA((nc - 1,))] * 2,
         compiler_params=pltpu.CompilerParams(
             collective_id=1, has_side_effects=True, vmem_limit_bytes=LIMIT
         ),
-    )(part.reshape(n, 8, cols))
-    return out.reshape(RANK, cols), sq.reshape(RANK, 128)
+    )(g, m, t)
+    return out.reshape(n, RANK, tile), sq
 
 
 def final_kernel(scale, g_ref, m_ref, w_ref, o_ref, rt_ref, sq_ref, nw_ref, nm_ref, nf_ref):
-    rt = rt_ref[...]
-    ft = rt / jnp.sqrt(sq_ref[:, :1] / COLS + 1e-06)
+    rt = jnp.concatenate([rt_ref[k] for k in range(rt_ref.shape[0])], axis=1)
+    ft = rt / jnp.sqrt(sq_ref[...].T[:, :1] / COLS + 1e-06)
     nf_ref[...] = ft.T
     buffer = g_ref[...].astype(F32) + m_ref[...].astype(F32)
     nm_ref[...] = (buffer - mm(o_ref[:, :RANK], ((1.0 - decay) * rt).astype(BF16))).astype(BF16)
@@ -481,8 +489,8 @@
             block,
             block,
             whole((rows, 3 * RANK)),
-            pl.BlockSpec((RANK, tile), lambda i: (0, i)),
-            whole((RANK, 128)),
+            pl.BlockSpec((tile // rt.shape[2], RANK, rt.shape[2]), lambda i: (i, 0, 0)),
+            whole((8, RANK)),
         ],
         out_specs=[block, block, pl.BlockSpec((tile, RANK), lambda i: (i, 0))],
         out_shape=[
@@ -498,7 +506,7 @@
     part = left_part(gradient, momentum, right_factor)
     left, gram = sums(part, nr, nc)
     o, t = ortho_of(gram, left)
-    rt, sq = right_total(right_part(gradient, momentum, t), nr, nc)
+    rt, sq = right_total(gradient, momentum, t, nr, nc)
     return tuple(final(gradient, momentum, weight, o, rt, sq))
 
 

time: 324 us -> 224 us (0.69)
  Pallas kernels: 323 us -> 222 us
    pallas_call x2 -> x1, Pallas kernels: 206 us -> 105 us  [right_total(): pl.pallas_call(functools.partial(right_kernel, nr, nc), in_specs=[hbm, hb...]
where the time goes in v3:
time: 224 us; the launch traced here: 223 us
  Pallas kernels  222 us (99%)
    pallas_call x1, Pallas kernels, right_total(): pl.pallas_call(functools.partial(right_kernel, nr, nc), in_specs=[hbm, hb...  105 us
    pallas_call x1, Pallas kernels, sums(): pl.pallas_call(functools.partial(sums_kernel, nr, nc), in_specs=[vm], out...  47.1 us
    pallas_call x1, Pallas kernels, final(): pl.pallas_call(functools.partial(final_kernel, step_size * (ROWS / RANK)...  34.5 us
    pallas_call x1, Pallas kernels, left_part(): pl.pallas_call(left_kernel, grid=(cols // tile,), in_specs=[pl.BlockSpec(...  22 us
    pallas_call x1, Pallas kernels, ortho_of(): pl.pallas_call(ortho_kernel, in_specs=[vm, vm], out_specs=[vm, vm], out_s...  13.6 us

profile of v3, /device:TPU:0, one launch (start us, length us, event | category | flops | bytes accessed | tf_op | source)
XLA Modules:
  0.0 222.7 jit_solution(1840885567751405342)
XLA Ops:
  0.6 22.0 %shard_map.67 = f32[1024,256]{1,0:T(8,128)} custom-call(bf16[1024,6656]{1,0:T(8,128)(2,1)} %g_ref.3, bf16[1024,6656]{1,0:T(8,128)(2,1)} %m_ref.3, f32[6656,256]{1,0:T(8,128)} %r_ref.1), custom_call_target="tpu_custom_call" | custom-call | tf_op jit(solution)/shard_map/pallas_call | solution.py:59
  22.6 47.1 %shard_map.68 = (f32[4,256,256]{2,1,0:T(8,128)}, f32[8,32,256]{2,1,0:T(8,128)}) custom-call(f32[4,256,256]{2,1,0:T(8,128)} %bitcast.5), custom_call_target="tpu_custom_call" | custom-call | tf_op jit(solution)/shard_map/pallas_call | solution.py:129
  69.7 13.6 %shard_map.69 = (bf16[1024,768]{1,0:T(8,128)(2,1)}, bf16[512,1024]{1,0:T(8,128)(2,1)}) custom-call(f32[256,256]{1,0:T(8,128)} %bitcast.7, f32[1024,256]{1,0:T(8,128)} %bitcast.6), custom_call_target="tpu_custom_call" | custom-call | tf_op jit(solution)/shard_map/pallas_call | solution.py:202
  83.4 104.8 %shard_map.70 = (f32[26,2,128,256]{3,2,1,0:T(8,128)}, f32[8,256]{1,0:T(8,128)}) custom-call(bf16[1024,6656]{1,0:T(8,128)(2,1)} %g_ref.3, bf16[1024,6656]{1,0:T(8,128)(2,1)} %m_ref.3, bf16[512,1024]{1,0:T(8,128)(2,1)} %get-tuple-element.12.t_ref), custom_call_target="tpu_custom_call" | custom-call | tf_op jit(solution)/shard_map/pallas_call | solution.py:441
  188.2 34.5 %shard_map.71 = (bf16[1024,6656]{1,0:T(8,128)(2,1)}, bf16[1024,6656]{1,0:T(8,128)(2,1)}, f32[6656,256]{1,0:T(8,128)}) custom-call(bf16[1024,6656]{1,0:T(8,128)(2,1)} %g_ref.3, bf16[1024,6656]{1,0:T(8,128)(2,1)} %m_ref.3, bf16[1024,6656]{1,0:T(8,128)(2,1)} %w_ref.1, bf16[1024,768]{1,0:T(8,128)(2,1)} %get-tuple-element.11.o_ref, f32[26,256,256]{2,1,0:T(8,128)} %bitcast.4, ...), custom_call_target="tpu_custom_call" | custom-call | tf_op jit(solution)/shard_map/pallas_call | solution.py:484

commit v4 on v3

--- a/solution.py
+++ b/solution.py
@@ -77,7 +77,7 @@
     return barrier
 
 
-def sums_kernel(nr, nc, part, left, gram, l_in, g_part, g_in, ls, lr, las, lar, gs, gr, gas, gar):
+def sums_kernel(nr, nc, part, left, gram, l_in, g_part, g_in, g_col, ls, lr, las, lar, gcs, gcr, gs, gr, gas, gar):
     ri, ci = lax.axis_index("row"), lax.axis_index("col")
     cols = [lax.rem(ci + d, nc) for d in range(nc)]
     rows = [lax.rem(ri + d, nr) for d in range(nr)]
@@ -89,37 +89,58 @@
             src_ref=src, dst_ref=dst, send_sem=send, recv_sem=recv, device_id=peer, device_id_type=MESH
         )
 
-    def reduce_gather(axis, n, me, others, src, slots, total, s1, r1, s2, r2):
-        first = [
-            copy(src.at[others[d]], slots.at[d - 1], s1.at[d - 1], r1.at[d - 1], {axis: others[d]})
+    def scatter(axis, n, others, src, slots, send, recv):
+        copies = [
+            copy(src.at[others[d]], slots.at[d - 1], send.at[d - 1], recv.at[d - 1], {axis: others[d]})
             for d in range(1, n)
         ]
-        for c in first:
+        for c in copies:
             c.start()
-        acc = src[me]
-        for d in range(1, n):
-            first[d - 1].wait_recv()
-            acc = acc + slots[d - 1]
-        total[me] = acc
-        second = [
-            copy(total.at[me], total.at[me], s2.at[d - 1], r2.at[d - 1], {axis: others[d]})
+        return copies
+
+    def gather(axis, n, me, others, total, send, recv):
+        copies = [
+            copy(total.at[me], total.at[me], send.at[d - 1], recv.at[d - 1], {axis: others[d]})
             for d in range(1, n)
         ]
-        for c in second:
+        for c in copies:
             c.start()
+        return copies
+
+    def gathered(axis, n, me, others, total, send, recv):
         for d in range(1, n):
             owner = lax.rem(me + n - d, n)
-            copy(total.at[owner], total.at[owner], s2.at[d - 1], r2.at[d - 1], {axis: others[d]}).wait_recv()
-        for c in first + second:
-            c.wait_send()
-
-    reduce_gather("col", nc, ci, cols, part, l_in, left, ls, lr, las, lar)
-    total = jnp.zeros((RANK, RANK), F32)
-    for k in range(nc):
-        block = left[k]
-        total += jnp.dot(block.T, block, precision=HIGH, preferred_element_type=F32)
-    g_part[...] = total.reshape(g_part.shape)
-    reduce_gather("row", nr, ri, rows, g_part, g_in, gram, gs, gr, gas, gar)
+            copy(total.at[owner], total.at[owner], send.at[d - 1], recv.at[d - 1], {axis: others[d]}).wait_recv()
+
+    def added(acc, copies, slots):
+        for d, c in enumerate(copies):
+            c.wait_recv()
+            acc = acc + slots[d]
+        return acc
+
+    sent = scatter("col", nc, cols, part, l_in, ls, lr)
+    block = added(part[ci], sent, l_in)
+    left[ci] = block
+    sent += gather("col", nc, ci, cols, left, las, lar)
+    product = jnp.dot(block.T, block, precision=HIGH, preferred_element_type=F32)
+    g_part[...] = product.reshape(g_part.shape)
+    over_row = scatter("row", nr, rows, g_part, g_in, gs, gr)
+    g_col[0] = added(g_part[ri], over_row, g_in)
+    over_col = [
+        copy(g_col.at[0], g_col.at[d], gcs.at[d - 1], gcr.at[d - 1], {"col": cols[d]}) for d in range(1, nc)
+    ]
+    for c in over_col:
+        c.start()
+    piece = g_col[0]
+    for d in range(1, nc):
+        over_col[d - 1].wait_recv()
+        piece = piece + g_col[d]
+    gram[ri] = piece
+    sent += over_row + over_col + gather("row", nr, ri, rows, gram, gas, gar)
+    gathered("row", nr, ri, rows, gram, gas, gar)
+    gathered("col", nc, ci, cols, left, las, lar)
+    for c in sent:
+        c.wait_send()
 
 
 def sums(part, nr, nc):
@@ -138,8 +159,9 @@
             VMEM((nc - 1, piece, RANK), F32),
             VMEM((nr, gpiece, RANK), F32),
             VMEM((nr - 1, gpiece, RANK), F32),
+            VMEM((nc, gpiece, RANK), F32),
         ]
-        + [DMA((nc - 1,))] * 4
+        + [DMA((nc - 1,))] * 6
         + [DMA((nr - 1,))] * 4,
         compiler_params=pltpu.CompilerParams(
             collective_id=0, has_side_effects=True, vmem_limit_bytes=LIMIT

time: 224 us -> 218 us (0.973)
  Pallas kernels: 222 us -> 216 us
    pallas_call x1, Pallas kernels: 47.1 us -> 41.9 us  [sums(): pl.pallas_call(functools.partial(sums_kernel, nr, nc), in_specs=[vm], out...]
where the time goes in v4:
time: 218 us; the launch traced here: 217 us
  Pallas kernels  216 us (99%)
    pallas_call x1, Pallas kernels, right_total(): pl.pallas_call(functools.partial(right_kernel, nr, nc), in_specs=[hbm, hb...  104 us
    pallas_call x1, Pallas kernels, sums(): pl.pallas_call(functools.partial(sums_kernel, nr, nc), in_specs=[vm], out...  41.9 us
    pallas_call x1, Pallas kernels, final(): pl.pallas_call(functools.partial(final_kernel, step_size * (ROWS / RANK)...  34.5 us
    pallas_call x1, Pallas kernels, left_part(): pl.pallas_call(left_kernel, grid=(cols // tile,), in_specs=[pl.BlockSpec(...  22 us
    pallas_call x1, Pallas kernels, ortho_of(): pl.pallas_call(ortho_kernel, in_specs=[vm, vm], out_specs=[vm, vm], out_s...  13.6 us

profile of v4, /device:TPU:0, one launch (start us, length us, event | category | flops | bytes accessed | tf_op | source)
XLA Modules:
  0.0 216.9 jit_solution(12855699590523872847)
XLA Ops:
  0.6 22.0 %shard_map.67 = f32[1024,256]{1,0:T(8,128)} custom-call(bf16[1024,6656]{1,0:T(8,128)(2,1)} %g_ref.3, bf16[1024,6656]{1,0:T(8,128)(2,1)} %m_ref.3, f32[6656,256]{1,0:T(8,128)} %r_ref.1), custom_call_target="tpu_custom_call" | custom-call | tf_op jit(solution)/shard_map/pallas_call | solution.py:59
  22.6 41.9 %shard_map.68 = (f32[4,256,256]{2,1,0:T(8,128)}, f32[8,32,256]{2,1,0:T(8,128)}) custom-call(f32[4,256,256]{2,1,0:T(8,128)} %bitcast.5), custom_call_target="tpu_custom_call" | custom-call | tf_op jit(solution)/shard_map/pallas_call | solution.py:150
  64.5 13.6 %shard_map.69 = (bf16[1024,768]{1,0:T(8,128)(2,1)}, bf16[512,1024]{1,0:T(8,128)(2,1)}) custom-call(f32[256,256]{1,0:T(8,128)} %bitcast.7, f32[1024,256]{1,0:T(8,128)} %bitcast.6), custom_call_target="tpu_custom_call" | custom-call | tf_op jit(solution)/shard_map/pallas_call | solution.py:224
  78.1 104.2 %shard_map.70 = (f32[26,2,128,256]{3,2,1,0:T(8,128)}, f32[8,256]{1,0:T(8,128)}) custom-call(bf16[1024,6656]{1,0:T(8,128)(2,1)} %g_ref.3, bf16[1024,6656]{1,0:T(8,128)(2,1)} %m_ref.3, bf16[512,1024]{1,0:T(8,128)(2,1)} %get-tuple-element.12.t_ref), custom_call_target="tpu_custom_call" | custom-call | tf_op jit(solution)/shard_map/pallas_call | solution.py:463
  182.3 34.5 %shard_map.71 = (bf16[1024,6656]{1,0:T(8,128)(2,1)}, bf16[1024,6656]{1,0:T(8,128)(2,1)}, f32[6656,256]{1,0:T(8,128)}) custom-call(bf16[1024,6656]{1,0:T(8,128)(2,1)} %g_ref.3, bf16[1024,6656]{1,0:T(8,128)(2,1)} %m_ref.3, bf16[1024,6656]{1,0:T(8,128)(2,1)} %w_ref.1, bf16[1024,768]{1,0:T(8,128)(2,1)} %get-tuple-element.11.o_ref, f32[26,256,256]{2,1,0:T(8,128)} %bitcast.4, ...), custom_call_target="tpu_custom_call" | custom-call | tf_op jit(solution)/shard_map/pallas_call | solution.py:506
